TPU v7x, 512 devices: a whole 4x8x8 slice. The times are simulated.
512 devices in a mesh: row: 16 (over y, core), col: 32 (over x, z).
Axes of the slice: x: 4, y: 8, z: 8, core: 2. Of those that a mesh axis runs over, the one named last changes fastest.
Arguments:
- diag_inverse: bfloat16 [2048, 2048], P(None, 'col'), as said below
- row_v: bfloat16 [16, 2048, 512], P('row', 'col'), may hold values from -0.8984375 to 0.8984375
- row_rank: int32 [16], P('row'), may hold values from 64 to 512, as said below
- col_v: bfloat16 [64, 2048, 512], P('col', 'row'), may hold values from -0.8984375 to 0.8984375
- col_rank: int32 [64], P('col'), may hold values from 64 to 512, as said below
Outputs:
- solved_v: bfloat16 [16, 2048, 512], P('row', 'col')
- coupling: bfloat16 [16, 64, 512, 512], P('row', 'col')
Inputs may be any that keep to these rules, and one draw needn't show every extreme that they name: `row_rank`: each rank is one of 64, 128, 256, 512; both the smallest and the largest occur. `col_rank`: each rank is one of 64, 128, 256, 512; both the smallest and the largest occur. `diag_inverse`: lower triangular with a diagonal between 0.5 and 2.
All inputs are finite; a program needn't handle non-finite values.
Results may differ from a plain program's by a relative error of at most 0.0055.
Values may be sent and summed in bfloat16 or wider, within the bound.
A program may use at most 64 MiB of HBM per device.

v0:
```python
import jax
import jax.numpy as jnp
from jax import lax
from jax.sharding import PartitionSpec as P


def on_device(diag_inverse, row_v, row_rank, col_v, col_rank):
    width = row_v.shape[2]
    places = jnp.arange(width, dtype=jnp.int32)
    nothing = jnp.zeros((), jnp.bfloat16)
    row_masked = jnp.where(places[None, None, :] < row_rank[:, None, None], row_v, nothing)
    col_masked = jnp.where(places[None, None, :] < col_rank[:, None, None], col_v, nothing)
    local_rows = row_masked[0]
    inner = (((0,), (0,)), ((), ()))
    block_rows = diag_inverse
    solved_local = lax.psum_scatter(
        jnp.dot(block_rows, local_rows, preferred_element_type=jnp.float32),
        "col",
        scatter_dimension=0,
        tiled=True,
    ).astype(jnp.bfloat16)
    block_rows = diag_inverse
    normal_rows = lax.dot_general(
        block_rows,
        lax.all_gather(solved_local, "col", axis=0, tiled=True),
        inner,
        preferred_element_type=jnp.float32,
    ).astype(jnp.bfloat16)
    panel_entire = lax.all_gather(col_masked, "row", axis=1, tiled=True)
    coupling = jnp.einsum(
        "nq,tnp->tqp",
        lax.all_gather(normal_rows, "col", axis=0, tiled=True),
        panel_entire,
        preferred_element_type=jnp.float32,
    )
    return (solved_local[None], coupling.astype(jnp.bfloat16)[None])


def solution(mesh):
    in_specs = (P(None, "col"), P("row", "col", None), P("row"), P("col", "row", None), P("col"))
    out_specs = (P("row", "col", None), P("row", "col", None, None))
    return jax.shard_map(
        on_device, mesh=mesh, in_specs=in_specs, out_specs=out_specs, check_vma=False
    )
```

profile of v0, /device:TPU:1, one launch (start us, length us, event | category | flops | bytes accessed | tf_op | source)
XLA Modules:
  0.0 482.8 jit_solution(8834529222203946482)
XLA Ops:
  7.2 0.0 copy-start
  7.2 0.0 reduce-scatter.4.cloned.1.call-start
  7.9 0.2 copy-done
  8.1 3.5 convolution_bitcast_fusion
  11.7 5.4 %copy.14 = f32[2048,512]{1,0:T(8,128)} copy(f32[2048,512]{0,1:T(8,128)} %convolution_bitcast_fusion) | data formatting | bytes 8388608
  17.0 0.0 copy-start.1
  17.0 0.0 copy-start.2
  17.0 0.0 reduce-scatter.4.cloned.1.call-update
  17.0 0.0 all-gather.6.cloned.1.call-start
  17.1 227.8 %reduce-scatter.4.cloned.1.call-done = f32[64,512]{1,0:T(8,128)} async-done(((f32[2048,512]{1,0:T(8,128)}), f32[64,512]{1,0:T(8,128)}) %reduce-scatter.4.cloned.1.call-update) | async-done | bytes 131088
  244.9 1.0 copy.15
  245.9 0.7 copy.11
  246.7 0.0 all-gather.6.cloned.1.call-update
  246.7 0.0 all-gather.4.cloned.1.call-start
  246.7 0.0 copy-done.1
  246.7 0.2 copy.10
  246.9 0.0 copy-done.2
  246.9 0.1 iota_compare_fusion
  247.0 0.9 broadcast_select_fusion
  247.9 0.0 all-gather.4.cloned.1.call-update
  247.9 0.0 all-gather.8.cloned.1.call-start
  248.0 84.0 %all-gather.6.cloned.1.call-done = bf16[2048,512]{1,0:T(8,128)(2,1)} async-done(((bf16[64,512]{1,0:T(8,128)(2,1)}), bf16[2048,512]{1,0:T(8,128)(2,1)}) %all-gather.6.cloned.1.call-update) | async-done | bytes 2097168 | tf_op jit(solution)/shard_map/all_gather | solution.py:25
  331.9 2.7 fusion.8
  334.6 0.0 all-gather.8.cloned.1.call-update
  334.7 0.7 copy.12
  335.4 53.3 %all-gather.4.cloned.1.call-done = bf16[2,2048,512]{1,2,0:T(8,128)(2,1)} async-done(((bf16[2,128,512]{1,2,0:T(8,128)(2,1)}), bf16[2,2048,512]{1,2,0:T(8,128)(2,1)}) %all-gather.4.cloned.1.call-update) | async-done | bytes 4194320 | tf_op jit(solution)/shard_map/all_gather | solution.py:29
  388.7 81.0 %all-gather.8.cloned.1.call-done = bf16[2048,512]{1,0:T(8,128)(2,1)} async-done(((bf16[64,512]{1,0:T(8,128)(2,1)}), bf16[2048,512]{1,0:T(8,128)(2,1)}) %all-gather.8.cloned.1.call-update) | async-done | bytes 2097168 | tf_op jit(solution)/shard_map/all_gather | solution.py:32
  469.7 5.2 %fusion.5 = bf16[1,2,512,512]{2,3,1,0:T(8,128)(2,1)S(1)} fusion(bf16[2,2048,512]{1,2,0:T(8,128)(2,1)} %all-gather.4.cloned.1.call-done, bf16[2048,512]{1,0:T(8,128)(2,1)} %all-gather.8.cloned.1.call-done), kind=kOutput, calls=%fused_computation.4 | convolution fusion | flops 2148007936 | bytes 7340032 | tf_op jit(solution)/shard_map/nq,tnp->tqp/dot_general | solution.py:30
  474.9 1.3 copy.13
  (1 shorter events, 0.0 us)
Async XLA Ops:
  7.2 1.0 copy-start
  7.2 237.7 %reduce-scatter.4.cloned.1.call-start = ((), (), s32[]{:S(2)}) async-start(), calls=%async_computation.4 | async-start | bytes 4325376
  17.0 229.7 %copy-start.1 = (bf16[2,128,512]{2,1,0:T(8,128)(2,1)S(1)}, bf16[2,128,512]{2,1,0:T(8,128)(2,1)}, u32[]{:S(2)}) copy-start(bf16[2,128,512]{2,1,0:T(8,128)(2,1)} %param.8) | copy-start | bytes 786436
  17.0 229.9 %copy-start.2 = (s32[2]{0:T(128)S(1)}, s32[2]{0:T(128)}, u32[]{:S(2)}) copy-start(s32[2]{0:T(128)} %param.9) | copy-start | bytes 28
  17.0 314.9 %all-gather.6.cloned.1.call-start = ((), (), s32[]{:S(2)}) async-start(), calls=%async_computation.2 | async-start | bytes 2162688 | tf_op jit(solution)/shard_map/all_gather | solution.py:25
  246.7 142.0 %all-gather.4.cloned.1.call-start = ((), (), s32[]{:S(2)}) async-start(), calls=%async_computation.1 | async-start | bytes 4456448 | tf_op jit(solution)/shard_map/all_gather | solution.py:29
  247.9 221.8 %all-gather.8.cloned.1.call-start = ((), (), s32[]{:S(2)}) async-start(), calls=%async_computation.3 | async-start | bytes 2162688 | tf_op jit(solution)/shard_map/all_gather | solution.py:32
Sparse Core Ops, SparseCore 0:
  17.2 227.6 reduce-scatter.3
  249.1 82.7 all-gather.5
  334.8 53.8 all-gather.3
  392.2 77.4 all-gather.7
where the time goes:
time: 486 us; the launch traced here: 483 us
  waiting for transfers between devices  446 us (92%)
  between operations  14.5 us (3%)
  matrix products  11.4 us (2%)
  local copies, waits for them, and re-layouts  9.56 us (2%)
    unnamed x5, waiting for transfers between devices  228 us
    all_gather x1, waiting for transfers between devices, on_device(): lax.all_gather(solved_local, 'col', axis=0, tiled=True)  84 us
    all_gather x1, waiting for transfers between devices, on_device(): lax.all_gather(normal_rows, 'col', axis=0, tiled=True)  81 us
    all_gather x1, waiting for transfers between devices, on_device(): panel_entire = lax.all_gather(col_masked, 'row', axis=1, tiled=True)  53.3 us
  transfers between devices with their start and end apart: 4, of which 4 were waited for; matrix products, arithmetic and copies ran while one was open for 1% of the time, Pallas kernels for 0%

commit v1 on v0

v1 whole, which is shorter than its diff:
```python
import functools

import jax
import jax.numpy as jnp
from jax import lax
from jax.experimental import pallas as pl
from jax.experimental.pallas import tpu as pltpu
from jax.sharding import PartitionSpec as P

MESH = pl.DeviceIdType.MESH
TILE = 2048
RANK = 512
NX, NY, NZ = 4, 8, 8
ROWS = TILE // (NX * NZ)
HALF = ROWS // 2
CROWS = TILE // (2 * NY)
STREAMS = "VDCK"


def names():
    out = []
    out += [("Vz", s, h) for s, n in (("L", 4), ("S", 3)) for h in range(1, n + 1)]
    out += [("Vx", s, k) for s in ("L1", "L2", "S1") for k in range(8)]
    out += [("Dx", s) for s in ("L1", "L2", "S1")]
    out += [("Dz", x0, s, h) for x0 in range(4) for s, n in (("L", 4), ("S", 3)) for h in range(1, n + 1)]
    out += [("Ds", x0, k) for x0 in range(4) for k in range(8)]
    out += [("Cy", s, h) for s, n in (("L", 4), ("S", 3)) for h in range(1, n + 1)]
    out += [("Cs", k) for k in range(8)]
    return {n: i for i, n in enumerate(out)}


SEM = names()
HOPS = [None, ("L", 1), ("S", 1), ("L", 2), ("S", 2), ("L", 3), ("S", 3), ("L", 4)]


def kernel(dt_in, v_in, c_in, s_out, k_out, dt, v, c, vt, st, nt, send_sem, recv_sem, local_sem):
    row = lax.axis_index("row")
    col = lax.axis_index("col")
    core = row % 2
    y = row // 2
    x = col // NZ
    z = col % NZ
    d = 1 - 2 * core

    def at_z(step):
        return row, x * NZ + (z + step + NZ) % NZ

    def at_x(step):
        return row, ((x + step + NX) % NX) * NZ + z

    def at_y(step):
        return ((y + step + NY) % NY) * 2 + core, col

    sibling = (y * 2 + 1 - core, col)

    barrier = pltpu.get_barrier_semaphore()
    peers = (at_z(1), at_z(-1), at_x(1), at_x(-1), at_y(1), at_y(-1), sibling)
    for peer in peers:
        pl.semaphore_signal(barrier, inc=1, device_id=peer, device_id_type=MESH)
    pl.semaphore_wait(barrier, len(peers))

    copies = {}

    def send(name, src, dst, to):
        i = SEM[name]
        copy = pltpu.make_async_remote_copy(
            src_ref=src, dst_ref=dst, send_sem=send_sem.at[i], recv_sem=recv_sem.at[i],
            device_id=to, device_id_type=MESH,
        )
        copy.start()
        copies[name] = copy

    def got(name):
        copies[name].wait_recv()

    def vblock(xx, zz):
        return v.at[pl.ds(pl.multiple_of((xx * NZ + zz) * ROWS, ROWS), ROWS)]

    def dblock(xx, zz, first=0):
        rows = pl.ds(pl.multiple_of((xx * NZ + zz) * ROWS + core * HALF, HALF), HALF)
        return dt.at[rows, first:]

    def cblock(yy):
        return c.at[:, pl.ds(pl.multiple_of((yy * 2 + core) * CROWS, CROWS), CROWS)]

    def zz_of(k):
        if HOPS[k] is None:
            return z
        s, h = HOPS[k]
        return (z - d * h + NZ) % NZ if s == "L" else (z + d * h + NZ) % NZ

    def yy_of(k):
        if HOPS[k] is None:
            return y
        s, h = HOPS[k]
        return (y - d * h + NY) % NY if s == "L" else (y + d * h + NY) % NY

    xm = (x - d + NX) % NX

    own_d = dt_in.at[pl.ds(pl.multiple_of(core * HALF, HALF), HALF)]
    local = [
        pltpu.make_async_copy(own_d, dblock(x, z), local_sem.at[0]),
        pltpu.make_async_copy(v_in, vblock(x, z), local_sem.at[1]),
        pltpu.make_async_copy(c_in, cblock(y), local_sem.at[2]),
    ]
    for copy in local:
        copy.start()

    if "D" in STREAMS:
        send(("Dx", "L1"), own_d, dblock(x, z), at_x(d))
        send(("Dx", "S1"), own_d, dblock(x, z), at_x(-d))
    if "V" in STREAMS:
        send(("Vz", "L", 1), v_in, vblock(x, z), at_z(d))
        send(("Vz", "S", 1), v_in, vblock(x, z), at_z(-d))
        send(("Vx", "L1", 0), v_in, vblock(x, z), at_x(d))
        send(("Vx", "S1", 0), v_in, vblock(x, z), at_x(-d))
    if "C" in STREAMS:
        send(("Cy", "L", 1), c_in, cblock(y), at_y(d))
        send(("Cy", "S", 1), c_in, cblock(y), at_y(-d))
        send(("Cs", 0), c_in, cblock(y), sibling)

    def v_z(k):
        s, h = HOPS[k]
        got(("Vz", s, h))
        zz = zz_of(k)
        if (s, h) not in (("L", 4), ("S", 3)):
            send(("Vz", s, h + 1), vblock(x, zz), vblock(x, zz), at_z(d if s == "L" else -d))
        send(("Vx", "L1", k), vblock(x, zz), vblock(x, zz), at_x(d))
        send(("Vx", "S1", k), vblock(x, zz), vblock(x, zz), at_x(-d))

    def v_x(k):
        got(("Vx", "L1", k))
        b = vblock(xm, zz_of(k))
        send(("Vx", "L2", k), b, b, at_x(d))

    def c_y(k):
        s, h = HOPS[k]
        got(("Cy", s, h))
        b = cblock(yy_of(k))
        if (s, h) not in (("L", 4), ("S", 3)):
            send(("Cy", s, h + 1), b, b, at_y(d if s == "L" else -d))
        send(("Cs", k), b, b, sibling)

    def d_x1():
        got(("Dx", "L1"))
        b = dblock(xm, z)
        send(("Dx", "L2"), b, b, at_x(d))

    def d_x2():
        got(("Dx", "S1"))
        got(("Dx", "L2"))
        for x0 in range(4):
            b = dblock(x0, z, 512 * x0)
            send(("Dz", x0, "L", 1), b, b, at_z(d))
            send(("Dz", x0, "S", 1), b, b, at_z(-d))
        for x0 in range(4):
            b = dblock(x0, z, 512 * x0)
            send(("Ds", x0, 0), b, b, sibling)

    def d_z(x0, k):
        s, h = HOPS[k]
        got(("Dz", x0, s, h))
        b = dblock(x0, zz_of(k), 512 * x0)
        if (s, h) not in (("L", 4), ("S", 3)):
            send(("Dz", x0, s, h + 1), b, b, at_z(d if s == "L" else -d))
        send(("Ds", x0, k), b, b, sibling)

    V, D, C = "V" in STREAMS, "D" in STREAMS, "C" in STREAMS
    for copy in local:
        copy.wait()
    if V:
        v_z(1), v_z(2)
    if D:
        d_x1()
    if V:
        v_z(3), v_z(4)
    if C:
        c_y(1), c_y(2)
    if V:
        v_x(0), v_x(1), v_x(2)
    if D:
        d_x2()
    if V:
        v_z(5), v_z(6), v_z(7)
        v_x(3), v_x(4)
    if D:
        for x0 in range(4):
            d_z(x0, 1), d_z(x0, 2)
    if C:
        c_y(3), c_y(4)
    if V:
        v_x(5), v_x(6), v_x(7)
    if D:
        for x0 in range(4):
            d_z(x0, 3), d_z(x0, 4)
    if C:
        c_y(5), c_y(6)
    if D:
        for x0 in range(4):
            d_z(x0, 5), d_z(x0, 6)
    if C:
        c_y(7)
    if D:
        for x0 in range(4):
            d_z(x0, 7)
    if V:
        for k in range(8):
            got(("Vx", "S1", k)), got(("Vx", "L2", k))
    if D:
        for x0 in range(4):
            for k in range(8):
                got(("Ds", x0, k))
    if C:
        for k in range(8):
            got(("Cs", k))

    if "K" in STREAMS:
        vt[...] = v[...].T

        for a in range(0, TILE, 256):
            e = a + 256
            st[:, a:e] = jnp.dot(
                vt[:, :e], dt[:e, a:e], preferred_element_type=jnp.float32
            ).astype(jnp.bfloat16)
        for a in range(0, TILE, 256):
            e = a + 256
            nt[:, a:e] = lax.dot_general(
                st[:, a:], dt[a:e, a:], (((1,), (1,)), ((), ())), preferred_element_type=jnp.float32
            ).astype(jnp.bfloat16)
        for j in range(2):
            for p in range(0, RANK, 256):
                k_out[j, :, p:p + 256] = jnp.dot(
                    nt[...], c[j, :, p:p + 256], preferred_element_type=jnp.float32
                ).astype(jnp.bfloat16)
        pair = pl.multiple_of((col // 2) * 2 * ROWS, 2 * ROWS)
        both = st[:, pl.ds(pair, 2 * ROWS)].T
        s_out[...] = jnp.where(col % 2 == 0, both[:ROWS], both[ROWS:])
    else:
        s_out[...] = v[:ROWS]
        k_out[...] = c[:, :RANK]

    for copy in copies.values():
        copy.wait_send()


def on_device(diag_inverse, row_v, row_rank, col_v, col_rank):
    vmem = pl.BlockSpec(memory_space=pltpu.VMEM)
    hbm = pl.BlockSpec(memory_space=pltpu.HBM)
    solved, cores = pl.pallas_call(
        kernel,
        out_shape=(
            jax.ShapeDtypeStruct((ROWS, RANK), jnp.bfloat16),
            jax.ShapeDtypeStruct((2, RANK, RANK), jnp.bfloat16),
        ),
        in_specs=[hbm] * 3,
        out_specs=(vmem, vmem),
        scratch_shapes=[
            pltpu.VMEM((TILE, TILE), jnp.bfloat16),
            pltpu.VMEM((TILE, RANK), jnp.bfloat16),
            pltpu.VMEM((2, TILE, RANK), jnp.bfloat16),
            pltpu.VMEM((RANK, TILE), jnp.bfloat16),
            pltpu.VMEM((RANK, TILE), jnp.bfloat16),
            pltpu.VMEM((RANK, TILE), jnp.bfloat16),
            pltpu.SemaphoreType.DMA((len(SEM),)),
            pltpu.SemaphoreType.DMA((len(SEM),)),
            pltpu.SemaphoreType.DMA((3,)),
        ],
        compiler_params=pltpu.CompilerParams(
            collective_id=0, has_side_effects=True, vmem_limit_bytes=48 * 1024 * 1024
        ),
    )(diag_inverse.T, row_v[0], col_v)
    places = jnp.arange(RANK, dtype=jnp.int32)
    nothing = jnp.zeros((), jnp.bfloat16)
    rows = places < row_rank[0]
    cols = places[None, :] < col_rank[:, None]
    solved = jnp.where(rows[None, :], solved, nothing)
    cores = jnp.where(rows[None, :, None] & cols[:, None, :], cores, nothing)
    return solved[None], cores[None]


def solution(mesh):
    in_specs = (P(None, "col"), P("row", "col", None), P("row"), P("col", "row", None), P("col"))
    out_specs = (P("row", "col", None), P("row", "col", None, None))
    return jax.shard_map(
        on_device, mesh=mesh, in_specs=in_specs, out_specs=out_specs, check_vma=False
    )
```

time: 486 us -> 71 us (0.15)
  waiting for transfers between devices: 446 us -> 0 us
  Pallas kernels: 0 us -> 64 us
  between operations: 14.5 us -> 1.3 us
  matrix products: 11.4 us -> 0 us
  local copies, waits for them, and re-layouts: 9.56 us -> 3.39 us
    unnamed x5 -> x0, waiting for transfers between devices: 228 us -> none
    all_gather x3 -> x0, waiting for transfers between devices: 218 us -> none  [the longest x1 84 us: on_device(): lax.all_gather(solved_local, 'col', axis=0, tiled=True)]
    pallas_call x0 -> x1, Pallas kernels: none -> 64 us  [on_device(): pl.pallas_call(kernel, out_shape=(jax.ShapeDtypeStruct((ROWS, RANK), jnp....]
    dot_general x3 -> x0, matrix products: 11.4 us -> none  [the longest x1 5.19 us: on_device(): jnp.einsum('nq,tnp->tqp', lax.all_gather(normal_rows, 'col', axis=0, tile...]
    unnamed x11 -> x8, local copies, waits for them, and re-layouts: 8.83 us -> 3.39 us
  transfers between devices with their start and end apart: 4 -> 0, of which waited for: 4 -> 0; matrix products, arithmetic and copies ran while one was open for 1% -> 0% of each run, Pallas kernels for 0% -> 0%
where the time goes in v1:
time: 71 us; the launch traced here: 70.8 us
  Pallas kernels  64 us (90%)
  local copies, waits for them, and re-layouts  3.39 us (5%)
  other arithmetic  2.06 us (3%)
  between operations  1.3 us (2%)
    pallas_call x1, Pallas kernels, on_device(): pl.pallas_call(kernel, out_shape=(jax.ShapeDtypeStruct((ROWS, RANK), jnp....  64 us
    unnamed x8, local copies, waits for them, and re-layouts  3.39 us
    broadcast_in_dim x2, other arithmetic, on_device(): return (solved[None], cores[None])  1.98 us

profile of v1, /device:TPU:1, one launch (start us, length us, event | category | flops | bytes accessed | tf_op | source)
XLA Modules:
  0.0 70.8 jit_solution(6480323018719420514)
XLA Ops:
  1.3 0.0 copy-start.3
  1.3 0.6 copy-done.3
  1.9 0.1 iota_compare_fusion
  2.0 0.0 copy-start
  2.0 0.9 %copy-done = bf16[2048,64]{0,1:T(8,128)(2,1)S(1)} copy-done((bf16[2048,64]{0,1:T(8,128)(2,1)S(1)}, bf16[2048,64]{0,1:T(8,128)(2,1)}, u32[]{:S(2)}) %copy-start) | copy-done | bytes 262168
  3.0 0.0 copy-start.1
  3.0 0.9 %copy-done.1 = bf16[2,128,512]{2,1,0:T(8,128)(2,1)S(1)} copy-done((bf16[2,128,512]{2,1,0:T(8,128)(2,1)S(1)}, bf16[2,128,512]{2,1,0:T(8,128)(2,1)}, u32[]{:S(2)}) %copy-start.1) | copy-done | bytes 262168
  3.9 0.0 copy-start.2
  3.9 0.8 %copy-done.2 = bf16[1,64,512]{2,1,0:T(8,128)(2,1)S(1)} copy-done((bf16[1,64,512]{2,1,0:T(8,128)(2,1)S(1)}, bf16[1,64,512]{2,1,0:T(8,128)(2,1)}, u32[]{:S(2)}) %copy-start.2) | copy-done | bytes 65560
  4.8 64.0 %shard_map.68 = (bf16[64,512]{1,0:T(8,128)(2,1)S(1)}, bf16[2,512,512]{2,1,0:T(8,128)(2,1)S(1)}) custom-call(bf16[64,2048]{1,0:T(8,128)(2,1)S(1)} %bitcast.8, bf16[64,512]{1,0:T(8,128)(2,1)S(1)} %bitcast.9, bf16[2,128,512]{2,1,0:T(8,128)(2,1)S(1)} %copy-done.1), custom_call_target="tpu_custom_call" | custom-call | tf_op jit(solution)/shard_map/pallas_call | solution.py:249
  68.8 0.6 select_bitcast_fusion
  69.4 1.3 %fusion = bf16[1,2,512,512]{3,2,1,0:T(8,128)(2,1)} fusion(bf16[2,512,512]{2,1,0:T(8,128)(2,1)S(1)} %get-tuple-element.5, pred[2,512]{1,0:T(4,128)(4,1)S(1)} %iota_compare_fusion, pred[512]{0:T(512)(128)(4,1)S(1)} %iota_compare_fusion.1), kind=kLoop, calls=%fused_computation.1 | loop fusion | flops 1048576 | bytes 2098688 | tf_op jit(solution)/shard_map/broadcast_in_dim | solution.py:278
  (1 shorter events, 0.0 us)
Async XLA Ops:
  1.3 0.7 copy-start.3
  2.0 0.9 %copy-start = (bf16[2048,64]{0,1:T(8,128)(2,1)S(1)}, bf16[2048,64]{0,1:T(8,128)(2,1)}, u32[]{:S(2)}) copy-start(bf16[2048,64]{0,1:T(8,128)(2,1)} %param.5) | copy-start | bytes 786436
  3.0 0.9 %copy-start.1 = (bf16[2,128,512]{2,1,0:T(8,128)(2,1)S(1)}, bf16[2,128,512]{2,1,0:T(8,128)(2,1)}, u32[]{:S(2)}) copy-start(bf16[2,128,512]{2,1,0:T(8,128)(2,1)} %c_in.1) | copy-start | bytes 786436
  3.9 0.8 %copy-start.2 = (bf16[1,64,512]{2,1,0:T(8,128)(2,1)S(1)}, bf16[1,64,512]{2,1,0:T(8,128)(2,1)}, u32[]{:S(2)}) copy-start(bf16[1,64,512]{2,1,0:T(8,128)(2,1)} %param.6) | copy-start | bytes 196612

commit v2 on v0

v2 whole, which is shorter than its diff:
```python
import jax
import jax.numpy as jnp
from jax import lax
from jax.experimental import pallas as pl
from jax.experimental.pallas import tpu as pltpu
from jax.sharding import PartitionSpec as P

MESH = pl.DeviceIdType.MESH
BF16 = jnp.bfloat16
F32 = jnp.float32
TILE = 2048
RANK = 512
NX, NY, NZ = 4, 8, 8
ROWS = TILE // (NX * NZ)
HALF = ROWS // 2
GROUP = TILE // NX
CROWS = TILE // (2 * NY)
TAIL = 384
BODY = TILE - TAIL
BODY_ROWS = TILE - GROUP
PIECES = 2
DIRECT = ()
HOPS = ((), ("L", 1), ("S", 1), ("L", 2), ("S", 2), ("L", 3), ("S", 3), ("L", 4))
WAYS = (("L", 4), ("S", 3))

ORDER = (
    1000, 1, 87, 68, 79, 24, 5, 1001, 72, -1, 2, 80, 9, 88, -35, -68, -34, 50, 69, -5, 54, 57, 6, 8, 25, -32, 10,
    -33, 61, 47, -72, 40, -79, 81, 43, 26, -87, -2, 3, 36, 89, 73, -6, -50, 11, -54, -69, -80, 7, 82, -57, 27, -88,
    55, -61, 58, 12, 62, -10, 18, -47, 70, -43, 44, 28, 90, -3, 51, 4, 13, -81, -73, 29, -8, -11, 83, 48, -40, -36,
    74, -58, -89, 37, -55, -7, 14, 16, -62, -82, 84, 30, 59, -12, -44, -70, 56, 63, -51, -9, 17, 52, 19, 41, 91, 71,
    -13, -4, 45, 31, 15, -83, -48, 49, 20, -59, 21, 85, -90, -37, 38, -74, -52, -63, 60, -14, 53, -84, -56, -71, 86,
    75, -41, 42, -45, -15, 46, -95, 2000, -91, 22, 23, 92, 2001, -38, 39, -60, 77, -85, -49, -53, 93, -75, 66, -86,
    76, -42, -46, 65, -93, -39, 64, 67, -96, -92, -65, -66, 2002, 2003, 94, -64, 2004, 2005, -77, 2006, 2008, -76,
    78, 2007, 2009, -67, -94, -78, 2010,
)
TASKS = tuple(("T", m) for m in range(NX)) + tuple((s, b) for b in range(NX - 1) for s in ("S", "N")) + (("P", 3),)


def copy_names():
    out = [("Vz", s, h) for s, n in WAYS for h in range(1, n + 1)]
    out += [("Vx", s, k) for s in ("L1", "L2", "S1") for k in range(NZ)]
    out += [("Dx", x0) for x0 in range(NX)]
    out += [("Dz", x0, s, h) for x0 in range(NX) for s, n in WAYS for h in range(1, n + 1)]
    out += [("Ds", x0) for x0 in range(NX)]
    out += [("Az", s, h) for s, n in WAYS for h in range(1, n + 1)]
    out += [("Ax", s) for s in ("L1", "L2", "S1")] + [("As", 0)]
    out += [("Cy", s, h, j) for s, n in WAYS for h in range(1, n + 1) for j in range(PIECES)]
    out += [("Cs", j) for j in range(PIECES)]
    out += [("Vx", "S1"), ("Vx", "L2")]
    return out


NAMES = [None] + copy_names()
SEM = {n: i - 1 for i, n in enumerate(NAMES) if i}
SENT = {"V": 0, "A": 1, "As": 2, "own": 3, "D": 4, "Cy": 8, "Cs": 10}
WIDE = 12


def kernel(
    dt_in, v_in, row_rank, c_in, col_rank_in, s_out, k_out, dt, v, c, vt, st, nt, na, sa, col_rank,
    send_sem, recv_sem, local_sem, rank_sem,
):
    row = lax.axis_index("row")
    col = lax.axis_index("col")
    core = lax.rem(row, 2)
    y = lax.div(row, 2)
    x = lax.div(col, NZ)
    z = lax.rem(col, NZ)
    d = 1 - 2 * core

    def around(at, step, n):
        return lax.rem(at + step + n, n)

    def at_z(step):
        return row, x * NZ + around(z, step, NZ)

    def at_x(step):
        return row, around(x, step, NX) * NZ + z

    def at_y(step):
        return around(y, step, NY) * 2 + core, col

    sibling = (y * 2 + 1 - core, col)
    to_z = {"L": at_z(d), "S": at_z(-d)}
    to_y = {"L": at_y(d), "S": at_y(-d)}
    to_x = {"L1": at_x(d), "L2": at_x(d), "S1": at_x(-d), "X2": at_x(2)}
    near_z, near_y = [z], [y]
    for s, h in HOPS[1:]:
        near_z.append(around(z, -d * h if s == "L" else d * h, NZ))
        near_y.append(around(y, -d * h if s == "L" else d * h, NY))
    x_from = (x, around(x, -d, NX), around(x, d, NX), around(x, 2, NX))

    barrier = pltpu.get_barrier_semaphore()
    peers = (*to_z.values(), to_x["L1"], to_x["S1"], to_x["X2"], *to_y.values(), sibling)
    for peer in peers:
        pl.semaphore_signal(barrier, inc=1, device_id=peer, device_id_type=MESH)
    pl.semaphore_wait(barrier, len(peers))

    half = pl.ds(pl.multiple_of(core * HALF, HALF), HALF)

    def body(x0):
        return pl.ds(GROUP * x0, BODY - GROUP * x0)

    tail = pl.ds(BODY, TAIL)

    def v_block(xx, zz):
        return v.at[pl.ds(pl.multiple_of((xx * NZ + zz) * ROWS, ROWS), ROWS)]

    def d_block(xx, zz, columns):
        return dt.at[xx * NZ + zz, half, columns]

    def c_block(yy, j):
        return c.at[j, yy, core] if PIECES == 2 else c.at[:, yy, core]

    def leaving(at, s, h):
        return at[0 if h == 1 else HOPS.index((s, h - 1))]

    def ends(name):
        kind = name[0]
        if kind == "Vz":
            s, h = name[1:]
            block = v_block(x, leaving(near_z, s, h))
            return (v_in if h == 1 else block), block, to_z[s], SENT["V"]
        if kind == "Vx":
            s, k = name[1:]
            if s == "L2" and k in DIRECT:
                s = "X2"
            block = v_block(x_from[1] if s == "L2" else x, near_z[k])
            return (v_in if k == 0 and s != "L2" else block), block, to_x[s], SENT["V"]
        if kind == "Dz":
            x0, s, h = name[1:]
            block = d_block(x0, leaving(near_z, s, h), body(x0))
            return block, block, to_z[s], SENT["D"] + x0
        if kind == "Ds":
            x0 = name[1]
            block = dt.at[pl.ds(x0 * NZ, NZ), half, body(x0)]
            return block, block, sibling, SENT["D"] + x0
        if kind == "Az":
            s, h = name[1:]
            block = d_block(x, leaving(near_z, s, h), tail)
            return (dt_in.at[half, tail] if h == 1 else block), block, to_z[s], SENT["A"]
        if kind == "Ax":
            s = name[1]
            xx = x_from[1] if s == "L2" else x
            block = dt.at[pl.ds(xx * NZ, NZ), half, tail]
            return block, block, to_x[s], SENT["A"]
        if kind == "As":
            block = dt.at[:, half, tail]
            return block, block, sibling, SENT["As"]
        if kind == "Cy":
            s, h, j = name[1:]
            block = c_block(leaving(near_y, s, h), j)
            src = block if h > 1 else (c_in.at[j] if PIECES == 2 else c_in)
            return src, block, to_y[s], SENT["Cy"] + j
        j = name[1]
        block = c.at[j, :, core] if PIECES == 2 else c.at[:, :, core]
        return block, block, sibling, SENT["Cs"] + j

    def arrival(name):
        if name[0] == "Vx" and name[1] in ("S1", "L2"):
            return recv_sem.at[SEM[name[:2]]]
        return recv_sem.at[SEM[name]]

    def start(name):
        src, dst, to, sent = ends(name)
        pltpu.make_async_remote_copy(
            src_ref=src, dst_ref=dst, send_sem=send_sem.at[sent], recv_sem=arrival(name),
            device_id=to, device_id_type=MESH,
        ).start()

    def wait_bytes(ref, sem):
        pltpu.make_async_copy(ref, ref, sem).wait()

    def wait(name):
        if len(name) == 2 and name[0] == "Vx":
            ref = v.at[pl.ds(0, NZ * ROWS)]
        elif name[0] == "Dx":
            ref = d_block(name[1], z, body(name[1]))
        else:
            ref = ends(name)[1]
        wait_bytes(ref, arrival(name))

    def start_own(x0, kind):
        src, dst = dt_in.at[half, body(x0)], d_block(x0, z, body(x0))
        if kind == "x":
            ways = [(to_x[s], SENT["own"], ("Dx", x0)) for s in ("L1", "S1", "X2")]
        else:
            ways = [(to_z[s], SENT["D"] + x0, ("Dz", x0, s, 1)) for s in ("L", "S")]
        for to, sent, name in ways:
            pltpu.make_async_remote_copy(
                src_ref=src, dst_ref=dst, send_sem=send_sem.at[sent], recv_sem=arrival(name),
                device_id=to, device_id_type=MESH,
            ).start()

    def finish_sends():
        wait_bytes(v.at[pl.ds(0, 31 * ROWS)], send_sem.at[SENT["V"]])
        for x0 in range(NX):
            wait_bytes(dt.at[pl.ds(0, 15), pl.ds(0, HALF), body(x0)], send_sem.at[SENT["D"] + x0])
        if TAIL:
            wait_bytes(dt.at[pl.ds(0, 31), pl.ds(0, HALF), tail], send_sem.at[SENT["A"]])
            wait_bytes(dt.at[:, half, tail], send_sem.at[SENT["As"]])
        for j in range(PIECES):
            ring = c.at[j, pl.ds(0, 7), 0] if PIECES == 2 else c.at[:, pl.ds(0, 7), 0]
            wait_bytes(ring, send_sem.at[SENT["Cy"] + j])
            across = c.at[j, :, core] if PIECES == 2 else c.at[:, :, core]
            wait_bytes(across, send_sem.at[SENT["Cs"] + j])
        for x0 in range(NX):
            only_here(
                x0, True,
                lambda x0=x0: wait_bytes(dt.at[pl.ds(0, 3), pl.ds(0, HALF), body(x0)], send_sem.at[SENT["own"]]),
            )

    local = [
        pltpu.make_async_copy(dt_in.at[half], d_block(x, z, pl.ds(0, TILE)), local_sem.at[0]),
        pltpu.make_async_copy(v_in, v_block(x, z), local_sem.at[1]),
    ]
    local += [
        pltpu.make_async_copy(c_in.at[j] if PIECES == 2 else c_in, c_block(y, j), local_sem.at[2 + j])
        for j in range(PIECES)
    ]

    ranks = [
        pltpu.make_async_copy(col_rank_in, col_rank, rank_sem.at[0]),
    ]

    def finish_local():
        for one in local:
            one.wait()

    def only_here(x0, here, make):
        @pl.when(x == x0 if here else x != x0)
        def _():
            make()

    def compute(task):
        kind, b = task
        if kind == "T":
            first = pl.multiple_of(x_from[b] * GROUP, GROUP)
            vt[:, pl.ds(first, GROUP)] = v[pl.ds(first, GROUP)].T
            return
        if kind == "P":
            for a in range(0, GROUP, 256):
                columns = dt[:BODY_ROWS // ROWS, :, BODY_ROWS + a:BODY_ROWS + a + 256]
                sa[:, a:a + 256] = jnp.dot(
                    vt[:, :BODY_ROWS], columns.reshape(BODY_ROWS, 256), preferred_element_type=F32
                )
            return
        lo, hi = GROUP * b, GROUP * (b + 1)
        if kind == "S":
            for a in range(lo, hi, 256):
                e = min(a + 256, hi)
                st[:, a:e] = jnp.dot(
                    vt[:, :hi], dt[:hi // ROWS, :, a:e].reshape(hi, e - a), preferred_element_type=F32
                ).astype(BF16)
            return
        for a in range(0, hi, 256):
            e = a + 256
            part = lax.dot_general(
                st[:, lo:hi], dt[a // ROWS:e // ROWS, :, lo:hi].reshape(256, GROUP),
                (((1,), (1,)), ((), ())), preferred_element_type=F32,
            )
            if b < NX - 1:
                na[:, a:e] = part if a >= lo else na[:, a:e] + part
            else:
                nt[:, a:e] = (part if a >= lo else na[:, a:e] + part).astype(BF16)

    def finish():
        for a in range(0, GROUP, 256):
            e = BODY_ROWS + a
            last = dt[BODY_ROWS // ROWS:, :, e:e + 256].reshape(GROUP, 256)
            part = jnp.dot(vt[:, BODY_ROWS:], last, preferred_element_type=F32)
            st[:, e:e + 256] = (sa[:, a:a + 256] + part).astype(BF16)
        compute(("N", NX - 1))
        pair = pl.multiple_of((col // 2) * 2 * ROWS, 2 * ROWS)
        both = st[:, pl.ds(pair, 2 * ROWS)].T
        mine = jnp.where(col % 2 == 0, both[:ROWS], both[ROWS:])
        for one in ranks:
            one.wait()
        q = lax.broadcasted_iota(jnp.int32, (ROWS, RANK), 1)
        s_out[...] = jnp.where(q < row_rank[0], mine.astype(F32), 0.0).astype(BF16)
        q = lax.broadcasted_iota(jnp.int32, (RANK, 256), 0)
        p = lax.broadcasted_iota(jnp.int32, (RANK, 256), 1)
        for j in range(2):
            for first in range(0, RANK, 256):
                columns = c[j, :, :, :, first:first + 256].reshape(TILE, 256)
                part = jnp.dot(nt[...], columns, preferred_element_type=F32)
                kept = (q < row_rank[0]) & (p < col_rank[j] - first)
                k_out[j, :, first:first + 256] = jnp.where(kept, part, 0.0).astype(BF16)

    here = False
    for code in ORDER:
        if code in (1000, 1001):
            for x0 in range(NX):
                only_here(x0, True, lambda x0=x0: start_own(x0, "xz"[code - 1000]))
        elif code >= 2000:
            compute(TASKS[code - 2000])
        elif code > 0:
            name = NAMES[code]
            if name[0] == "Dz" and name[3] == 1:
                only_here(name[1], False, lambda name=name: start(name))
            else:
                start(name)
        else:
            if not here:
                for one in local + ranks:
                    one.start()
                finish_local()
                here = True
            name = NAMES[-code]
            if name[0] == "Dx":
                only_here(name[1], False, lambda name=name: wait(name))
            else:
                wait(name)

    finish()
    finish_sends()


VMEM_LIMIT = 48 * 1024 * 1024


def in_hbm(array):
    return pltpu.with_memory_space_constraint(array, pltpu.HBM)


def on_device(diag_inverse, row_v, row_rank, col_v, col_rank):
    vmem = pl.BlockSpec(memory_space=pltpu.VMEM)
    hbm = pl.BlockSpec(memory_space=pltpu.HBM)
    smem = pl.BlockSpec(memory_space=pltpu.SMEM)
    solved, cores = pl.pallas_call(
        kernel,
        out_shape=(
            pltpu.VMEM((ROWS, RANK), BF16),
            pltpu.VMEM((2, RANK, RANK), BF16),
        ),
        in_specs=[hbm, hbm, smem, hbm, hbm],
        out_specs=(vmem, vmem),
        scratch_shapes=[
            pltpu.VMEM((NX * NZ, ROWS, TILE), BF16),
            pltpu.VMEM((TILE, RANK), BF16),
            pltpu.VMEM((2, NY, 2, CROWS, RANK), BF16),
            pltpu.VMEM((RANK, TILE), BF16),
            pltpu.VMEM((RANK, TILE), BF16),
            pltpu.VMEM((RANK, TILE), BF16),
            pltpu.VMEM((RANK, TILE), F32),
            pltpu.VMEM((RANK, GROUP), F32),
            pltpu.SMEM((2,), jnp.int32),
            pltpu.SemaphoreType.DMA((WIDE,)),
            pltpu.SemaphoreType.DMA((len(SEM),)),
            pltpu.SemaphoreType.DMA((4,)),
            pltpu.SemaphoreType.DMA((1,)),
        ],
        compiler_params=pltpu.CompilerParams(
            collective_id=0, has_side_effects=True, vmem_limit_bytes=VMEM_LIMIT
        ),
    )(in_hbm(diag_inverse.T), in_hbm(row_v[0]), row_rank, in_hbm(col_v), in_hbm(col_rank))
    return solved[None], cores[None]


def solution(mesh):
    in_specs = (P(None, "col"), P("row", "col", None), P("row"), P("col", "row", None), P("col"))
    out_specs = (P("row", "col", None), P("row", "col", None, None))
    return jax.shard_map(
        on_device, mesh=mesh, in_specs=in_specs, out_specs=out_specs, check_vma=False
    )
```

time: 486 us -> 58.1 us (0.12)
  waiting for transfers between devices: 446 us -> 0 us
  Pallas kernels: 0 us -> 55 us
  between operations: 14.5 us -> 1.28 us
  matrix products: 11.4 us -> 0 us
  local copies, waits for them, and re-layouts: 9.56 us -> 1.6 us
    unnamed x5 -> x0, waiting for transfers between devices: 228 us -> none
    all_gather x3 -> x0, waiting for transfers between devices: 218 us -> none  [the longest x1 84 us: on_device(): lax.all_gather(solved_local, 'col', axis=0, tiled=True)]
    pallas_call x0 -> x1, Pallas kernels: none -> 55 us  [on_device(): pl.pallas_call(kernel, out_shape=(pltpu.VMEM((ROWS, RANK), BF16), pltpu.V...]
    dot_general x3 -> x0, matrix products: 11.4 us -> none  [the longest x1 5.19 us: on_device(): jnp.einsum('nq,tnp->tqp', lax.all_gather(normal_rows, 'col', axis=0, tile...]
    unnamed x11 -> x2, local copies, waits for them, and re-layouts: 8.83 us -> 1.6 us
  transfers between devices with their start and end apart: 4 -> 0, of which waited for: 4 -> 0; matrix products, arithmetic and copies ran while one was open for 1% -> 0% of each run, Pallas kernels for 0% -> 0%
where the time goes in v2:
time: 58.1 us; the launch traced here: 57.9 us
  Pallas kernels  55 us (95%)
  local copies, waits for them, and re-layouts  1.6 us (3%)
  between operations  1.28 us (2%)
    pallas_call x1, Pallas kernels, on_device(): pl.pallas_call(kernel, out_shape=(pltpu.VMEM((ROWS, RANK), BF16), pltpu.V...  55 us
    unnamed x2, local copies, waits for them, and re-layouts  1.6 us

profile of v2, /device:TPU:1, one launch (start us, length us, event | category | flops | bytes accessed | tf_op | source)
XLA Modules:
  0.0 57.9 jit_solution(17584034036941975739)
XLA Ops:
  1.3 55.0 %shard_map.68 = (bf16[64,512]{1,0:T(8,128)(2,1)S(1)}, bf16[2,512,512]{2,1,0:T(8,128)(2,1)S(1)}) custom-call(bf16[64,2048]{1,0:T(8,128)(2,1)} %bitcast.6, bf16[64,512]{1,0:T(8,128)(2,1)} %bitcast.7, s32[1]{0:T(128)S(6)} %copy.11.row_rank, bf16[2,128,512]{2,1,0:T(8,128)(2,1)} %c_in.1, s32[2]{0:T(128)} %col_rank_in.1), custom_call_target="tpu_custom_call" | custom-call | tf_op jit(solution)/shard_map/pallas_call | solution.py:330
  56.3 0.6 %copy.9 = bf16[1,64,512]{2,1,0:T(8,128)(2,1)} copy(bf16[1,64,512]{2,1,0:T(8,128)(2,1)S(1)} %bitcast.5) | data formatting | bytes 131072
  57.0 1.0 %copy.10 = bf16[1,2,512,512]{3,2,1,0:T(8,128)(2,1)} copy(bf16[1,2,512,512]{3,2,1,0:T(8,128)(2,1)S(1)} %bitcast.4) | data formatting | bytes 2097152

commit v3 on v2

--- a/solution.py
+++ b/solution.py
@@ -19,19 +19,19 @@
 BODY = TILE - TAIL
 BODY_ROWS = TILE - GROUP
 PIECES = 2
-DIRECT = ()
+DIRECT = (0, 7,)
 HOPS = ((), ("L", 1), ("S", 1), ("L", 2), ("S", 2), ("L", 3), ("S", 3), ("L", 4))
 WAYS = (("L", 4), ("S", 3))
 
 ORDER = (
-    1000, 1, 87, 68, 79, 24, 5, 1001, 72, -1, 2, 80, 9, 88, -35, -68, -34, 50, 69, -5, 54, 57, 6, 8, 25, -32, 10,
-    -33, 61, 47, -72, 40, -79, 81, 43, 26, -87, -2, 3, 36, 89, 73, -6, -50, 11, -54, -69, -80, 7, 82, -57, 27, -88,
-    55, -61, 58, 12, 62, -10, 18, -47, 70, -43, 44, 28, 90, -3, 51, 4, 13, -81, -73, 29, -8, -11, 83, 48, -40, -36,
-    74, -58, -89, 37, -55, -7, 14, 16, -62, -82, 84, 30, 59, -12, -44, -70, 56, 63, -51, -9, 17, 52, 19, 41, 91, 71,
-    -13, -4, 45, 31, 15, -83, -48, 49, 20, -59, 21, 85, -90, -37, 38, -74, -52, -63, 60, -14, 53, -84, -56, -71, 86,
-    75, -41, 42, -45, -15, 46, -95, 2000, -91, 22, 23, 92, 2001, -38, 39, -60, 77, -85, -49, -53, 93, -75, 66, -86,
-    76, -42, -46, 65, -93, -39, 64, 67, -96, -92, -65, -66, 2002, 2003, 94, -64, 2004, 2005, -77, 2006, 2008, -76,
-    78, 2007, 2009, -67, -94, -78, 2010,
+    1000, 1, 24, 87, 68, 79, 16, 88, 5, 80, 1001, 72, -35, 61, 57, -1, 2, 9, -34, 50, -5, 6, 10, 8, -68, 54, -33,
+    69, 43, 25, -32, -87, 36, 89, -79, -57, 26, 58, -72, 40, 81, 47, -2, 3, 73, 11, -80, -6, 82, 28, -69, 12, 7,
+    -50, 51, -9, -61, -88, 90, 62, -10, -43, 18, 27, 70, -36, 17, 44, 37, -47, -58, -11, 19, -89, -81, 83, -3, 4,
+    -40, -54, 29, 59, 13, -73, -51, 48, -62, -12, 41, -82, 84, -90, 20, -70, 74, -7, 92, 71, 30, -44, 14, 45, 63,
+    91, 55, -37, 52, -4, 31, 38, -59, 23, 15, -83, 85, -13, -41, -48, 42, -71, -74, 75, 49, 21, -55, -45, -14, 46,
+    -84, -8, 86, -38, 39, 22, -92, -15, -52, 53, -63, -95, 2000, 77, -91, 56, -42, -85, 93, 60, 2002, -49, -46, 65,
+    -75, 76, -39, 64, -93, -53, 2001, -56, -65, -60, -86, 67, -96, 2003, 66, 94, -64, 2004, 2005, 2006, -66, -77,
+    2008, -76, 78, 2007, -67, -94, 2009, -78, 2010,
 )
 TASKS = tuple(("T", m) for m in range(NX)) + tuple((s, b) for b in range(NX - 1) for s in ("S", "N")) + (("P", 3),)
 

time: 58.1 us -> 56.7 us (0.976)
  Pallas kernels: 55 us -> 53.7 us
    pallas_call x1, Pallas kernels: 55 us -> 53.7 us  [on_device(): pl.pallas_call(kernel, out_shape=(pltpu.VMEM((ROWS, RANK), BF16), pltpu.V...]
where the time goes in v3:
time: 56.7 us; the launch traced here: 56.6 us
  Pallas kernels  53.7 us (95%)
  local copies, waits for them, and re-layouts  1.6 us (3%)
  between operations  1.28 us (2%)
    pallas_call x1, Pallas kernels, on_device(): pl.pallas_call(kernel, out_shape=(pltpu.VMEM((ROWS, RANK), BF16), pltpu.V...  53.7 us
    unnamed x2, local copies, waits for them, and re-layouts  1.6 us

profile of v3, /device:TPU:1, one launch (start us, length us, event | category | flops | bytes accessed | tf_op | source)
XLA Modules:
  0.0 56.6 jit_solution(14242502182213967212)
XLA Ops:
  1.3 53.7 %shard_map.68 = (bf16[64,512]{1,0:T(8,128)(2,1)S(1)}, bf16[2,512,512]{2,1,0:T(8,128)(2,1)S(1)}) custom-call(bf16[64,2048]{1,0:T(8,128)(2,1)} %bitcast.6, bf16[64,512]{1,0:T(8,128)(2,1)} %bitcast.7, s32[1]{0:T(128)S(6)} %copy.11.row_rank, bf16[2,128,512]{2,1,0:T(8,128)(2,1)} %c_in.1, s32[2]{0:T(128)} %col_rank_in.1), custom_call_target="tpu_custom_call" | custom-call | tf_op jit(solution)/shard_map/pallas_call | solution.py:330
  55.0 0.6 %copy.9 = bf16[1,64,512]{2,1,0:T(8,128)(2,1)} copy(bf16[1,64,512]{2,1,0:T(8,128)(2,1)S(1)} %bitcast.5) | data formatting | bytes 131072
  55.6 1.0 %copy.10 = bf16[1,2,512,512]{3,2,1,0:T(8,128)(2,1)} copy(bf16[1,2,512,512]{3,2,1,0:T(8,128)(2,1)S(1)} %bitcast.4) | data formatting | bytes 2097152

commit v4 on v3

--- a/solution.py
+++ b/solution.py
@@ -25,13 +25,13 @@
 
 ORDER = (
     1000, 1, 24, 87, 68, 79, 16, 88, 5, 80, 1001, 72, -35, 61, 57, -1, 2, 9, -34, 50, -5, 6, 10, 8, -68, 54, -33,
-    69, 43, 25, -32, -87, 36, 89, -79, -57, 26, 58, -72, 40, 81, 47, -2, 3, 73, 11, -80, -6, 82, 28, -69, 12, 7,
-    -50, 51, -9, -61, -88, 90, 62, -10, -43, 18, 27, 70, -36, 17, 44, 37, -47, -58, -11, 19, -89, -81, 83, -3, 4,
-    -40, -54, 29, 59, 13, -73, -51, 48, -62, -12, 41, -82, 84, -90, 20, -70, 74, -7, 92, 71, 30, -44, 14, 45, 63,
-    91, 55, -37, 52, -4, 31, 38, -59, 23, 15, -83, 85, -13, -41, -48, 42, -71, -74, 75, 49, 21, -55, -45, -14, 46,
-    -84, -8, 86, -38, 39, 22, -92, -15, -52, 53, -63, -95, 2000, 77, -91, 56, -42, -85, 93, 60, 2002, -49, -46, 65,
-    -75, 76, -39, 64, -93, -53, 2001, -56, -65, -60, -86, 67, -96, 2003, 66, 94, -64, 2004, 2005, 2006, -66, -77,
-    2008, -76, 78, 2007, -67, -94, 2009, -78, 2010,
+    69, 43, 25, -32, 36, -57, 26, -87, 89, 58, -72, -79, 40, 81, 47, -2, 3, 73, 11, -6, 28, -69, -80, 82, 12, 7,
+    -50, 51, -9, -61, 62, -10, -43, -88, 90, 18, 27, 70, -36, 17, 44, 37, -47, -58, -11, 19, -3, 4, -40, -89, -81,
+    83, -54, 29, 59, 13, -73, -51, 48, -62, -12, 41, 20, -70, 74, -82, 84, -7, -90, 92, 71, 30, -44, 14, 45, 63, 91,
+    55, -37, 52, -4, 31, 38, -59, 23, 15, -13, -41, -48, -83, 85, 42, -71, -74, 75, 49, 21, -55, -45, -14, 46, -8,
+    -38, 39, -84, 86, 22, -15, -52, 53, -63, -92, -95, 2000, 77, 56, -42, 60, -91, 2002, -49, -85, 93, -46, 65, -75,
+    76, -39, 64, -93, -53, 2001, -56, -65, -60, 67, -96, 2003, 66, -86, 94, -64, 2004, 2005, 2006, -66, -77, 2008,
+    -76, 78, 2007, -67, -94, 2009, -78, 2010,
 )
 TASKS = tuple(("T", m) for m in range(NX)) + tuple((s, b) for b in range(NX - 1) for s in ("S", "N")) + (("P", 3),)
 
@@ -240,23 +240,25 @@
             return
         if kind == "P":
             for a in range(0, GROUP, 256):
-                columns = dt[:BODY_ROWS // ROWS, :, BODY_ROWS + a:BODY_ROWS + a + 256]
-                sa[:, a:a + 256] = jnp.dot(
-                    vt[:, :BODY_ROWS], columns.reshape(BODY_ROWS, 256), preferred_element_type=F32
-                )
+                total = None
+                for m in range(NX - 1):
+                    part = last_columns(m, a)
+                    total = part if total is None else total + part
+                sa[:, a:a + 256] = total
             return
         lo, hi = GROUP * b, GROUP * (b + 1)
         if kind == "S":
             for a in range(lo, hi, 256):
-                e = min(a + 256, hi)
+                e = a + 256
                 st[:, a:e] = jnp.dot(
-                    vt[:, :hi], dt[:hi // ROWS, :, a:e].reshape(hi, e - a), preferred_element_type=F32
+                    vt[:, :e], dt[:e // ROWS, :, a:e].reshape(e, 256), preferred_element_type=F32
                 ).astype(BF16)
             return
         for a in range(0, hi, 256):
             e = a + 256
+            k = max(lo, a)
             part = lax.dot_general(
-                st[:, lo:hi], dt[a // ROWS:e // ROWS, :, lo:hi].reshape(256, GROUP),
+                st[:, k:hi], dt[a // ROWS:e // ROWS, :, k:hi].reshape(256, hi - k),
                 (((1,), (1,)), ((), ())), preferred_element_type=F32,
             )
             if b < NX - 1:
@@ -264,12 +266,15 @@
             else:
                 nt[:, a:e] = (part if a >= lo else na[:, a:e] + part).astype(BF16)
 
+    def last_columns(m, a):
+        first = pl.multiple_of(x_from[m] * GROUP, GROUP)
+        columns = dt[pl.ds(x_from[m] * NZ, NZ), :, BODY_ROWS + a:BODY_ROWS + a + 256]
+        return jnp.dot(vt[:, pl.ds(first, GROUP)], columns.reshape(GROUP, 256), preferred_element_type=F32)
+
     def finish():
         for a in range(0, GROUP, 256):
             e = BODY_ROWS + a
-            last = dt[BODY_ROWS // ROWS:, :, e:e + 256].reshape(GROUP, 256)
-            part = jnp.dot(vt[:, BODY_ROWS:], last, preferred_element_type=F32)
-            st[:, e:e + 256] = (sa[:, a:a + 256] + part).astype(BF16)
+            st[:, e:e + 256] = (sa[:, a:a + 256] + last_columns(NX - 1, a)).astype(BF16)
         compute(("N", NX - 1))
         pair = pl.multiple_of((col // 2) * 2 * ROWS, 2 * ROWS)
         both = st[:, pl.ds(pair, 2 * ROWS)].T

time: 56.7 us -> 56.5 us (level)
  no operation moved by 1% of the time
where the time goes in v4:
time: 56.5 us; the launch traced here: 56.4 us
  Pallas kernels  53.5 us (95%)
  local copies, waits for them, and re-layouts  1.6 us (3%)
  between operations  1.28 us (2%)
    pallas_call x1, Pallas kernels, on_device(): pl.pallas_call(kernel, out_shape=(pltpu.VMEM((ROWS, RANK), BF16), pltpu.V...  53.5 us
    unnamed x2, local copies, waits for them, and re-layouts  1.6 us

profile of v4, /device:TPU:1, one launch (start us, length us, event | category | flops | bytes accessed | tf_op | source)
XLA Modules:
  0.0 56.4 jit_solution(14061030349070396664)
XLA Ops:
  1.3 53.5 %shard_map.68 = (bf16[64,512]{1,0:T(8,128)(2,1)S(1)}, bf16[2,512,512]{2,1,0:T(8,128)(2,1)S(1)}) custom-call(bf16[64,2048]{1,0:T(8,128)(2,1)} %bitcast.6, bf16[64,512]{1,0:T(8,128)(2,1)} %bitcast.7, s32[1]{0:T(128)S(6)} %copy.11.row_rank, bf16[2,128,512]{2,1,0:T(8,128)(2,1)} %c_in.1, s32[2]{0:T(128)} %col_rank_in.1), custom_call_target="tpu_custom_call" | custom-call | tf_op jit(solution)/shard_map/pallas_call | solution.py:335
  54.8 0.6 %copy.9 = bf16[1,64,512]{2,1,0:T(8,128)(2,1)} copy(bf16[1,64,512]{2,1,0:T(8,128)(2,1)S(1)} %bitcast.5) | data formatting | bytes 131072
  55.4 1.0 %copy.10 = bf16[1,2,512,512]{3,2,1,0:T(8,128)(2,1)} copy(bf16[1,2,512,512]{3,2,1,0:T(8,128)(2,1)S(1)} %bitcast.4) | data formatting | bytes 2097152

commit v5 on v4

--- a/solution.py
+++ b/solution.py
@@ -30,8 +30,8 @@
     83, -54, 29, 59, 13, -73, -51, 48, -62, -12, 41, 20, -70, 74, -82, 84, -7, -90, 92, 71, 30, -44, 14, 45, 63, 91,
     55, -37, 52, -4, 31, 38, -59, 23, 15, -13, -41, -48, -83, 85, 42, -71, -74, 75, 49, 21, -55, -45, -14, 46, -8,
     -38, 39, -84, 86, 22, -15, -52, 53, -63, -92, -95, 2000, 77, 56, -42, 60, -91, 2002, -49, -85, 93, -46, 65, -75,
-    76, -39, 64, -93, -53, 2001, -56, -65, -60, 67, -96, 2003, 66, -86, 94, -64, 2004, 2005, 2006, -66, -77, 2008,
-    -76, 78, 2007, -67, -94, 2009, -78, 2010,
+    76, 1003, -39, 64, -93, -53, 2001, -56, -65, -60, 67, -96, 2003, 66, -86, 94, -64, 2004, 2005, 2006, -66, -77,
+    2008, -76, 78, 2007, -67, -94, 2009, -78, 2010,
 )
 TASKS = tuple(("T", m) for m in range(NX)) + tuple((s, b) for b in range(NX - 1) for s in ("S", "N")) + (("P", 3),)
 
@@ -293,12 +293,24 @@
                 k_out[j, :, first:first + 256] = jnp.where(kept, part, 0.0).astype(BF16)
 
     here = False
-    for code in ORDER:
+    passed = False
+    for position, code in enumerate(ORDER):
         if code in (1000, 1001):
             for x0 in range(NX):
                 only_here(x0, True, lambda x0=x0: start_own(x0, "xz"[code - 1000]))
+        elif code == 1003:
+            late = [b for b in ORDER[:position] if b >= 2000]
+
+            @pl.when(z > EARLY)
+            def _():
+                for b in late:
+                    compute(TASKS[b - 2000])
+
+            passed = True
+        elif code >= 2000 and passed:
+            compute(TASKS[code - 2000])
         elif code >= 2000:
-            compute(TASKS[code - 2000])
+            pl.when(z <= EARLY)(lambda code=code: compute(TASKS[code - 2000]))
         elif code > 0:
             name = NAMES[code]
             if name[0] == "Dz" and name[3] == 1:
@@ -321,6 +333,7 @@
     finish_sends()
 
 
+EARLY = 1
 VMEM_LIMIT = 48 * 1024 * 1024
 
 

time: 56.5 us -> 56.5 us (level)
  no operation moved by 1% of the time
where the time goes in v5:
time: 56.5 us; the launch traced here: 56.4 us
  Pallas kernels  53.5 us (95%)
  local copies, waits for them, and re-layouts  1.6 us (3%)
  between operations  1.28 us (2%)
    pallas_call x1, Pallas kernels, on_device(): pl.pallas_call(kernel, out_shape=(pltpu.VMEM((ROWS, RANK), BF16), pltpu.V...  53.5 us
    unnamed x2, local copies, waits for them, and re-layouts  1.6 us

profile of v5, /device:TPU:1, one launch (start us, length us, event | category | flops | bytes accessed | tf_op | source)
XLA Modules:
  0.0 56.4 jit_solution(2965162264151136334)
XLA Ops:
  1.3 53.5 %shard_map.68 = (bf16[64,512]{1,0:T(8,128)(2,1)S(1)}, bf16[2,512,512]{2,1,0:T(8,128)(2,1)S(1)}) custom-call(bf16[64,2048]{1,0:T(8,128)(2,1)} %bitcast.6, bf16[64,512]{1,0:T(8,128)(2,1)} %bitcast.7, s32[1]{0:T(128)S(6)} %copy.11.row_rank, bf16[2,128,512]{2,1,0:T(8,128)(2,1)} %c_in.1, s32[2]{0:T(128)} %col_rank_in.1), custom_call_target="tpu_custom_call" | custom-call | tf_op jit(solution)/shard_map/pallas_call | solution.py:348
  54.8 0.6 %copy.9 = bf16[1,64,512]{2,1,0:T(8,128)(2,1)} copy(bf16[1,64,512]{2,1,0:T(8,128)(2,1)S(1)} %bitcast.5) | data formatting | bytes 131072
  55.4 1.0 %copy.10 = bf16[1,2,512,512]{3,2,1,0:T(8,128)(2,1)} copy(bf16[1,2,512,512]{3,2,1,0:T(8,128)(2,1)S(1)} %bitcast.4) | data formatting | bytes 2097152
